TPU v7x, 256 devices: a whole 4x4x8 slice. The times are simulated.
256 devices in a mesh: row: 16 (over y, x_hi, core), col: 16 (over x_lo, z).
Axes of the slice: x: 4 (x_hi: 2, x_lo: 2; x = x_hi * 2 + x_lo), y: 4, z: 8, core: 2. Of those that a mesh axis runs over, the one named last changes fastest.
Arguments:
- tokens: bfloat16 [1024, 8192], P('col', 'row'), may hold values from -6 to 6
- cotangent: bfloat16 [1024, 8192], P('col', 'row'), may hold values from -6 to 6
- gate_weight: bfloat16 [8192, 16384], P('row', 'col'), may hold values from -0.0625 to 0.0625
- up_weight: bfloat16 [8192, 16384], P('row', 'col'), may hold values from -0.0625 to 0.0625
- down_weight: bfloat16 [16384, 8192], P('col', 'row'), may hold values from -0.046875 to 0.046875
Outputs:
- token_grad: float32 [1024, 8192], P('col', 'row')
- gate_grad: float32 [8192, 16384], P('row', 'col')
- up_grad: float32 [8192, 16384], P('row', 'col')
- down_grad: float32 [16384, 8192], P('col', 'row')
All inputs are finite; a program needn't handle non-finite values.
Results may differ from a plain program's by a relative error of at most 0.0029.
Values may be sent and summed in bfloat16 or wider, within the bound.
No kernel may reach another device: no remote copies, remote signals or barrier semaphores. Data moves between devices by JAX's collectives and lax.ppermute only.
A program may use at most 64 MiB of HBM per device.

v0:
```python
import jax
import jax.numpy as jnp
from jax import lax
from jax.sharding import PartitionSpec as P


def contract_last(left, right):
    return lax.dot_general(
        left, right, (((1,), (1,)), ((), ())), preferred_element_type=jnp.float32
    )


def contract_first(left, right):
    return lax.dot_general(
        left, right, (((0,), (0,)), ((), ())), preferred_element_type=jnp.float32
    )


def shards(tokens, cotangent, gate_weight, up_weight, down_weight):
    features, grads_in = (
        lax.all_gather(tokens, "col", axis=0, tiled=True),
        lax.all_gather(cotangent, "col", axis=0, tiled=True),
    )
    width = gate_weight.shape[1]
    paired = jnp.concatenate([gate_weight, up_weight], axis=1)
    rows = features
    joined = lax.psum_scatter(
        jnp.dot(rows, paired, preferred_element_type=jnp.float32),
        "row",
        scatter_dimension=0,
        tiled=True,
    )
    gate = joined[:, :width]
    up = joined[:, width:]
    sigma = jax.nn.sigmoid(gate)
    silu_gate = gate * sigma
    hidden = (silu_gate * up).astype(jnp.bfloat16)
    hidden_all = lax.all_gather(hidden, "row", axis=0, tiled=True)
    rows = grads_in
    hidden_grad = lax.psum_scatter(
        contract_last(rows, down_weight), "row", scatter_dimension=0, tiled=True
    )
    pre_gate = (hidden_grad * up * sigma * (1.0 + gate * (1.0 - sigma))).astype(jnp.bfloat16)
    pre_up = (hidden_grad * silu_gate).astype(jnp.bfloat16)
    gate_all, up_all = (
        lax.all_gather(pre_gate, "row", axis=0, tiled=True),
        lax.all_gather(pre_up, "row", axis=0, tiled=True),
    )
    down_grad = contract_first(hidden_all, grads_in)
    gate_grad = contract_first(features, gate_all)
    up_grad = contract_first(features, up_all)
    token_grad = lax.psum_scatter(
        contract_last(gate_all, gate_weight) + contract_last(up_all, up_weight),
        "col",
        scatter_dimension=0,
        tiled=True,
    )
    return (token_grad, gate_grad, up_grad, down_grad)


def solution(mesh):
    return jax.shard_map(
        shards,
        mesh=mesh,
        in_specs=(
            P("col", "row"),
            P("col", "row"),
            P("row", "col"),
            P("row", "col"),
            P("col", "row"),
        ),
        out_specs=(P("col", "row"), P("row", "col"), P("row", "col"), P("col", "row")),
        check_vma=False,
    )
```

profile of v0, /device:TPU:8, one launch (start us, length us, event | category | flops | bytes accessed | tf_op | source)
XLA Modules:
  0.0 602.5 jit_solution(16079564675103651573)
XLA Ops:
  7.2 0.0 all-gather.6.cloned.1.call-start
  7.2 0.7 all-gather.6.cloned.1.call-update
  7.9 0.0 all-gather.8.cloned.1.call-start
  8.0 0.7 all-gather.8.cloned.1.call-update
  8.7 0.0 reduce-scatter.4.cloned.1.call-start
  8.7 73.2 %all-gather.6.cloned.1.call-done = bf16[1024,512]{1,0:T(8,128)(2,1)} async-done(((bf16[64,512]{1,0:T(8,128)(2,1)}), bf16[1024,512]{1,0:T(8,128)(2,1)}) %all-gather.6.cloned.1.call-update) | async-done | bytes 1048592 | tf_op jit(solution)/shard_map/all_gather | solution.py:22
  81.9 4.5 fusion.5
  86.4 0.0 reduce-scatter.4.cloned.1.call-update
  86.4 0.0 reduce-scatter.6.cloned.1.call-start
  86.5 63.9 %all-gather.8.cloned.1.call-done = bf16[1024,512]{1,0:T(8,128)(2,1)} async-done(((bf16[64,512]{1,0:T(8,128)(2,1)}), bf16[1024,512]{1,0:T(8,128)(2,1)}) %all-gather.8.cloned.1.call-update) | async-done | bytes 1048592 | tf_op jit(solution)/shard_map/all_gather | solution.py:21
  150.4 6.8 %convolution_bitcast_fusion = f32[1024,2048]{1,0:T(8,128)} fusion(bf16[1024,512]{1,0:T(8,128)(2,1)} %all-gather.8.cloned.1.call-done, bf16[512,1024]{1,0:T(8,128)(2,1)S(1)} %copy-done.2, bf16[512,1024]{1,0:T(8,128)(2,1)S(1)} %copy-done.1), kind=kOutput, calls=%fused_computation | convolution fusion | flops 2151677952 | bytes 11534336 | tf_op jit(solution)/shard_map/dot_general | solution.py:28
  157.2 0.0 all-gather.10.cloned.1.call-start
  157.3 82.8 %reduce-scatter.4.cloned.1.call-done = f32[64,1024]{1,0:T(8,128)} async-done(((f32[1024,1024]{1,0:T(8,128)}), f32[64,1024]{1,0:T(8,128)}) %reduce-scatter.4.cloned.1.call-update) | async-done | bytes 262160 | tf_op jit(solution)/shard_map/reduce_scatter | solution.py:40
  240.1 114.1 %reduce-scatter.6.cloned.1.call-done = f32[64,2048]{1,0:T(8,128)} async-done(((f32[1024,2048]{1,0:T(8,128)}), f32[64,2048]{1,0:T(8,128)}) %reduce-scatter.6.cloned.1.call-update) | async-done | bytes 524304 | tf_op jit(solution)/shard_map/reduce_scatter | solution.py:27
  354.1 2.0 multiply_convert_fusion.1
  356.1 0.0 all-gather.10.cloned.1.call-update
  356.1 0.0 all-gather.12.cloned.1.call-start
  356.2 0.5 all-gather.12.cloned.1.call-update
  356.7 0.0 all-gather.14.cloned.1.call-start
  356.8 0.7 all-gather.14.cloned.1.call-update
  357.5 0.0 reduce-scatter.8.cloned.1.call-start
  357.5 51.7 %all-gather.10.cloned.1.call-done = bf16[1024,1024]{1,0:T(8,128)(2,1)} async-done(((bf16[64,1024]{1,0:T(8,128)(2,1)}), bf16[1024,1024]{1,0:T(8,128)(2,1)}) %all-gather.10.cloned.1.call-update) | async-done | bytes 2097168 | tf_op jit(solution)/shard_map/all_gather | solution.py:46
  409.2 4.2 fusion.6
  413.4 50.9 %all-gather.12.cloned.1.call-done = bf16[1024,1024]{1,0:T(8,128)(2,1)} async-done(((bf16[64,1024]{1,0:T(8,128)(2,1)}), bf16[1024,1024]{1,0:T(8,128)(2,1)}) %all-gather.12.cloned.1.call-update) | async-done | bytes 2097168 | tf_op jit(solution)/shard_map/all_gather | solution.py:47
  464.2 4.8 convolution_add_fusion
  469.1 3.1 convolution_bitcast_fusion.2
  472.2 1.8 copy.10
  474.0 3.1 convolution_bitcast_fusion.1
  477.2 1.8 copy.11
  479.0 39.9 %all-gather.14.cloned.1.call-done = bf16[1024,1024]{1,0:T(8,128)(2,1)} async-done(((bf16[64,1024]{1,0:T(8,128)(2,1)}), bf16[1024,1024]{1,0:T(8,128)(2,1)}) %all-gather.14.cloned.1.call-update) | async-done | bytes 2097168 | tf_op jit(solution)/shard_map/all_gather | solution.py:38
  518.8 4.5 fusion.7
  523.3 72.3 %reduce-scatter.8.cloned.1.call-done = f32[64,512]{1,0:T(8,128)} async-done(((f32[1024,512]{1,0:T(8,128)}), f32[64,512]{1,0:T(8,128)}) %reduce-scatter.8.cloned.1.call-update) | async-done | bytes 131088 | tf_op jit(solution)/shard_map/reduce_scatter | solution.py:52
  (8 shorter events, 0.0 us)
Async XLA Ops:
  7.2 74.8 %copy-start = (bf16[1024,512]{1,0:T(8,128)(2,1)S(1)}, bf16[1024,512]{1,0:T(8,128)(2,1)}, u32[]{:S(2)}) copy-start(bf16[1024,512]{1,0:T(8,128)(2,1)} %param.9) | copy-start | bytes 3145732
  7.2 74.8 %all-gather.6.cloned.1.call-start = ((), (), s32[]{:S(2)}) async-start(), calls=%async_computation.3 | async-start | bytes 1114112 | tf_op jit(solution)/shard_map/all_gather | solution.py:22
  7.9 142.5 %all-gather.8.cloned.1.call-start = ((), (), s32[]{:S(2)}) async-start(), calls=%async_computation.5 | async-start | bytes 1114112 | tf_op jit(solution)/shard_map/all_gather | solution.py:21
  8.7 231.4 %reduce-scatter.4.cloned.1.call-start = ((), (), s32[]{:S(2)}) async-start(), calls=%async_computation.4 | async-start | bytes 4456448 | tf_op jit(solution)/shard_map/reduce_scatter | solution.py:40
  86.4 64.0 %copy-start.1 = (bf16[512,1024]{1,0:T(8,128)(2,1)S(1)}, bf16[512,1024]{1,0:T(8,128)(2,1)}, u32[]{:S(2)}) copy-start(bf16[512,1024]{1,0:T(8,128)(2,1)} %param.7) | copy-start | bytes 3145732
  86.4 64.0 %copy-start.2 = (bf16[512,1024]{1,0:T(8,128)(2,1)S(1)}, bf16[512,1024]{1,0:T(8,128)(2,1)}, u32[]{:S(2)}) copy-start(bf16[512,1024]{1,0:T(8,128)(2,1)} %param.8) | copy-start | bytes 3145732
  86.4 267.7 %reduce-scatter.6.cloned.1.call-start = ((), (), s32[]{:S(2)}) async-start(), calls=%async_computation.6 | async-start | bytes 8912896 | tf_op jit(solution)/shard_map/reduce_scatter | solution.py:27
  157.2 252.0 %all-gather.10.cloned.1.call-start = ((), (), s32[]{:S(2)}) async-start(), calls=%async_computation.7 | async-start | bytes 2228224 | tf_op jit(solution)/shard_map/all_gather | solution.py:46
  356.1 108.1 %all-gather.12.cloned.1.call-start = ((), (), s32[]{:S(2)}) async-start(), calls=%async_computation.8 | async-start | bytes 2228224 | tf_op jit(solution)/shard_map/all_gather | solution.py:47
  356.7 162.1 %all-gather.14.cloned.1.call-start = ((), (), s32[]{:S(2)}) async-start(), calls=%async_computation.10 | async-start | bytes 2228224 | tf_op jit(solution)/shard_map/all_gather | solution.py:38
  357.5 238.2 %reduce-scatter.8.cloned.1.call-start = ((), (), s32[]{:S(2)}) async-start(), calls=%async_computation.9 | async-start | bytes 2228224 | tf_op jit(solution)/shard_map/reduce_scatter | solution.py:52
Sparse Core Ops, SparseCore 0:
  9.8 72.0 all-gather.5
  83.7 66.6 all-gather.7
  154.7 85.3 reduce-scatter.3
  245.1 108.9 reduce-scatter.5
  357.7 51.4 all-gather.9
  412.7 51.4 all-gather.11
  467.4 51.4 all-gather.13
  522.1 73.4 reduce-scatter.7
where the time goes:
time: 603 us; the launch traced here: 602 us
  waiting for transfers between devices  551 us (91%)
  matrix products  31 us (5%)
  between operations  14.2 us (2%)
    reduce_scatter x1, waiting for transfers between devices, shards(): lax.psum_scatter(jnp.dot(rows, paired, preferred_element_type=jnp.float32...  114 us
    reduce_scatter x1, waiting for transfers between devices, shards(): lax.psum_scatter(contract_last(rows, down_weight), 'row', scatter_dimensi...  82.8 us
    all_gather x1, waiting for transfers between devices, shards(): lax.all_gather(cotangent, 'col', axis=0, tiled=True)  73.2 us
    reduce_scatter x1, waiting for transfers between devices, shards(): lax.psum_scatter(contract_last(gate_all, gate_weight) + contract_last(up_...  72.3 us
    all_gather x1, waiting for transfers between devices, shards(): lax.all_gather(tokens, 'col', axis=0, tiled=True)  63.9 us
    all_gather x1, waiting for transfers between devices, shards(): lax.all_gather(pre_gate, 'row', axis=0, tiled=True)  51.7 us
    all_gather x1, waiting for transfers between devices, shards(): lax.all_gather(pre_up, 'row', axis=0, tiled=True)  50.9 us
    all_gather x1, waiting for transfers between devices, shards(): hidden_all = lax.all_gather(hidden, 'row', axis=0, tiled=True)  39.9 us
  transfers between devices with their start and end apart: 8, of which 8 were waited for; matrix products, arithmetic and copies ran while one was open for 6% of the time, Pallas kernels for 0%

commit v1 on v0

v1 whole, which is shorter than its diff:
```python
import jax
import jax.numpy as jnp
from jax import lax
from jax.experimental import pallas as pl
from jax.experimental.pallas import tpu as pltpu
from jax.sharding import Mesh, PartitionSpec as P

BF = jnp.bfloat16
F32 = jnp.float32
SIZES = {"y": 4, "h": 2, "c": 2, "l": 2, "z": 8}


def hop(x, axis, step=1):
    n = SIZES[axis]
    return lax.ppermute(x, axis, [(i, (i + step) % n) for i in range(n)])


def ring(x):
    up, down = [x], [x]
    for _ in range(3):
        up.append(hop(up[-1], "z", 1))
        down.append(hop(down[-1], "z", -1))
    half = x.shape[0] // 2
    far = jnp.concatenate([hop(up[3][:half], "z", 1), hop(down[3][half:], "z", -1)])
    return up + [far] + down[:0:-1]


def encode(v):
    v = v * 16.0
    s = v * jnp.abs(v)
    t = v * v
    return (s * t * (t * t)).astype(BF)


def decode(code):
    y = code.astype(F32)
    q = lax.rsqrt(lax.rsqrt(jnp.maximum(jnp.abs(y), 1e-37)))
    t = q * lax.rsqrt(q) * (1.0 / 16.0)
    return jnp.where(y == 0.0, 0.0, jnp.where(y < 0.0, -t, t))


def place_kernel(spot_ref, *refs):
    blocks, (feat, grad, sems) = refs[:16], refs[16:]
    copies = []
    for i in range(16):
        start = pl.multiple_of(spot_ref[i] * 64, 64)
        for j, out in enumerate((feat, grad)):
            copies.append(
                pltpu.make_async_copy(
                    blocks[i].at[pl.ds(64 * j, 64)],
                    out.at[pl.ds(start, 64)],
                    sems.at[2 * i + j],
                )
            )
    for copy in copies:
        copy.start()
    for copy in copies:
        copy.wait()


def place(blocks, spots):
    shape = jax.ShapeDtypeStruct((1024, 512), BF)
    return pl.pallas_call(
        place_kernel,
        out_shape=(shape, shape),
        in_specs=[pl.BlockSpec(memory_space=pltpu.SMEM)]
        + [pl.BlockSpec(memory_space=pl.ANY)] * 16,
        out_specs=[pl.BlockSpec(memory_space=pl.ANY)] * 2,
        scratch_shapes=[pltpu.SemaphoreType.DMA((32,))],
        name="place",
    )(spots, *blocks)


def dot_nn(a, b):
    return jnp.dot(a, b, preferred_element_type=F32)


def dot_nt(a, b):
    return lax.dot_general(a, b, (((1,), (1,)), ((), ())), preferred_element_type=F32)


def dot_tn(a, b):
    return lax.dot_general(a, b, (((0,), (0,)), ((), ())), preferred_element_type=F32)


def shards(tokens, cotangent, gate_weight, up_weight, down_weight):
    core, near, z = lax.axis_index("c"), lax.axis_index("l"), lax.axis_index("z")
    mine = jnp.concatenate([tokens, cotangent])
    blocks = ring(mine) + ring(hop(mine, "l"))
    where = jnp.arange(16)
    from_l, from_z = (near + where // 8) % 2, (z - where % 8) % 8
    spots = ((from_l + core) % 2) * 8 + from_z
    features, grads = place(blocks, spots.astype(jnp.int32))

    def sums(half):
        f, g = features[half], grads[half]
        return [dot_nn(f, gate_weight), dot_nn(f, up_weight), dot_nt(g, down_weight)]

    keep, send = slice(0, 512), slice(512, 1024)
    theirs = hop(jnp.concatenate([encode(v) for v in sums(send)], axis=1), "c")
    both = jnp.concatenate(sums(keep), axis=1) + decode(theirs)
    parts = lax.all_to_all(encode(both), ("y", "h"), 0, 0, tiled=True)
    total = decode(parts).reshape(8, 64, 3072).sum(0)
    gate, up, hidden_grad = total[:, :1024], total[:, 1024:2048], total[:, 2048:]
    sigma = jax.nn.sigmoid(gate)
    silu_gate = gate * sigma
    hidden = (silu_gate * up).astype(BF)
    pre_gate = (hidden_grad * up * sigma * (1.0 + gate * (1.0 - sigma))).astype(BF)
    pre_up = (hidden_grad * silu_gate).astype(BF)
    own = jnp.concatenate([hidden, pre_gate, pre_up], axis=1)
    ours = lax.all_to_all(
        jnp.broadcast_to(own[None], (8, 64, 3072)).reshape(512, 3072), ("y", "h"), 0, 0, tiled=True
    )
    every = jnp.concatenate([ours, hop(ours, "c")])
    hidden_all, gate_all, up_all = every[:, :1024], every[:, 1024:2048], every[:, 2048:]
    token_part = (dot_nt(gate_all, gate_weight) + dot_nt(up_all, up_weight)).astype(BF)
    twice = jnp.concatenate([token_part, token_part[:512]])
    token_part = lax.dynamic_slice(twice, (core * 512, 0), (1024, 512))
    token_parts = lax.all_to_all(token_part, ("l", "z"), 0, 0, tiled=True)
    token_grad = token_parts.astype(F32).reshape(16, 64, 512).sum(0)
    return (
        token_grad,
        dot_tn(features, gate_all),
        dot_tn(features, up_all),
        dot_tn(hidden_all, grads),
    )


def solution(mesh):
    fine = Mesh(mesh.devices.reshape(4, 2, 2, 2, 8), ("y", "h", "c", "l", "z"))
    row, col = ("y", "h", "c"), ("l", "z")
    return jax.shard_map(
        shards,
        mesh=fine,
        in_specs=(P(col, row), P(col, row), P(row, col), P(row, col), P(col, row)),
        out_specs=(P(col, row), P(row, col), P(row, col), P(col, row)),
        check_vma=False,
    )
```

time: 603 us -> 263 us (0.44)
  waiting for transfers between devices: 551 us -> 31 us
  blocking collectives: 0 us -> 87.4 us
  Pallas kernels: 0 us -> 65.6 us
  starting transfers between devices: 0.32 us -> 36.2 us
  other arithmetic: 1.98 us -> 16.2 us
  between operations: 14.2 us -> 1.07 us
  matrix products: 31 us -> 21.7 us
    all_gather x5 -> x0, waiting for transfers between devices: 280 us -> none  [the longest x1 73.2 us: shards(): lax.all_gather(cotangent, 'col', axis=0, tiled=True)]
    reduce_scatter x3 -> x0, waiting for transfers between devices: 269 us -> none  [the longest x1 114 us: shards(): lax.psum_scatter(jnp.dot(rows, paired, preferred_element_type=jnp.float32...]
    all_to_all x0 -> x2, blocking collectives: none -> 87.4 us  [the longest x1 45.4 us: shards(): parts = lax.all_to_all(encode(both), ('y', 'h'), 0, 0, tiled=True)]
    pallas_call x0 -> x1, Pallas kernels: none -> 65.6 us  [place(): pl.pallas_call(place_kernel, out_shape=(shape, shape), in_specs=[pl.Block...]
    ppermute x0 -> x19, starting transfers between devices: none -> 31.9 us  [hop(): return lax.ppermute(x, axis, [(i, (i + step) % n) for i in range(n)])]
    all_to_all x0 -> x1, waiting for transfers between devices: none -> 16.4 us  [shards(): token_parts = lax.all_to_all(token_part, ('l', 'z'), 0, 0, tiled=True)]
    ppermute x0 -> x19, waiting for transfers between devices: none -> 14.6 us  [hop(): return lax.ppermute(x, axis, [(i, (i + step) % n) for i in range(n)])]
    dot_general x7 -> x11, matrix products: 31 us -> 21.7 us  [the longest x3 11.3 us: dot_tn(): lax.dot_general(a, b, (((0,), (0,)), ((), ())), preferred_element_type=F32)]
  transfers between devices with their start and end apart: 8 -> 20, of which waited for: 8 -> 6; matrix products, arithmetic and copies ran while one was open for 6% -> 6% of each run, Pallas kernels for 0% -> 0%
where the time goes in v1:
time: 263 us; the launch traced here: 262 us
  blocking collectives  87.4 us (33%)
  Pallas kernels  65.6 us (25%)
  starting transfers between devices  36.2 us (14%)
  waiting for transfers between devices  31 us (12%)
  matrix products  21.7 us (8%)
  other arithmetic  16.2 us (6%)
  local copies, waits for them, and re-layouts  2.86 us (1%)
    pallas_call x1, Pallas kernels, place(): pl.pallas_call(place_kernel, out_shape=(shape, shape), in_specs=[pl.Block...  65.6 us
    all_to_all x1, blocking collectives, shards(): parts = lax.all_to_all(encode(both), ('y', 'h'), 0, 0, tiled=True)  45.4 us
    all_to_all x1, blocking collectives, shards(): lax.all_to_all(jnp.broadcast_to(own[None], (8, 64, 3072)).reshape(512, 30...  42 us
    ppermute x19, starting transfers between devices, hop(): return lax.ppermute(x, axis, [(i, (i + step) % n) for i in range(n)])  31.9 us
    all_to_all x1, waiting for transfers between devices, shards(): token_parts = lax.all_to_all(token_part, ('l', 'z'), 0, 0, tiled=True)  16.4 us
    ppermute x19, waiting for transfers between devices, hop(): return lax.ppermute(x, axis, [(i, (i + step) % n) for i in range(n)])  14.6 us
    dot_general x3, matrix products, dot_tn(): lax.dot_general(a, b, (((0,), (0,)), ((), ())), preferred_element_type=F32)  11.3 us
    dot_general x4, matrix products, dot_nt(): lax.dot_general(a, b, (((1,), (1,)), ((), ())), preferred_element_type=F32)  5.8 us
  transfers between devices with their start and end apart: 20, of which 6 were waited for; matrix products, arithmetic and copies ran while one was open for 6% of the time, Pallas kernels for 0%

profile of v1, /device:TPU:8, one launch (start us, length us, event | category | flops | bytes accessed | tf_op | source)
XLA Modules:
  0.0 262.1 jit_solution(2121476493897009337)
XLA Ops:
  0.6 0.9 constant_dynamic-update-slice_fusion.1
  2.4 1.5 collective-permute-start.8
  3.9 5.9 %collective-permute-start.4 = (bf16[128,512]{1,0:T(8,128)(2,1)S(1)}, bf16[128,512]{1,0:T(8,128)(2,1)S(1)}, u32[]{:S(2)}, u32[]{:S(2)}) collective-permute-start(bf16[128,512]{1,0:T(8,128)(2,1)S(1)} %constant_dynamic-update-slice_fusion.refs_0_), channel_id=1, source_target_pairs={{0,7},{1,0},{2,1},{3,2},{4,3},{5,4},{6,5},{7,6},{8,15},{9,8},{10,9... | collective-permute-start | bytes 393224 | tf_op jit(solution)/shard_map/ppermute | solution.py:15
  9.8 3.7 %collective-permute-start.13 = (bf16[128,512]{1,0:T(8,128)(2,1)S(1)}, bf16[128,512]{1,0:T(8,128)(2,1)S(1)}, u32[]{:S(2)}, u32[]{:S(2)}) collective-permute-start(bf16[128,512]{1,0:T(8,128)(2,1)S(1)} %collective-permute-done.8.refs_8_), channel_id=1, source_target_pairs={{0,7},{1,0},{2,1},{3,2},{4,3},{5,4},{6,5},{7,6},{8,15},{9,8},{10,9... | collective-permute-start | bytes 393224 | tf_op jit(solution)/shard_map/ppermute | solution.py:15
  13.5 3.2 %collective-permute-start.5 = (bf16[128,512]{1,0:T(8,128)(2,1)S(1)}, bf16[128,512]{1,0:T(8,128)(2,1)S(1)}, u32[]{:S(2)}, u32[]{:S(2)}) collective-permute-start(bf16[128,512]{1,0:T(8,128)(2,1)S(1)} %collective-permute-done.4.refs_7_), channel_id=1, source_target_pairs={{0,7},{1,0},{2,1},{3,2},{4,3},{5,4},{6,5},{7,6},{8,15},{9,8},{10,9... | collective-permute-start | bytes 393224 | tf_op jit(solution)/shard_map/ppermute | solution.py:15
  16.8 3.7 %collective-permute-start.14 = (bf16[128,512]{1,0:T(8,128)(2,1)S(1)}, bf16[128,512]{1,0:T(8,128)(2,1)S(1)}, u32[]{:S(2)}, u32[]{:S(2)}) collective-permute-start(bf16[128,512]{1,0:T(8,128)(2,1)S(1)} %collective-permute-done.13.refs_15_), channel_id=1, source_target_pairs={{0,7},{1,0},{2,1},{3,2},{4,3},{5,4},{6,5},{7,6},{8,15},{9,8},{10,9... | collective-permute-start | bytes 393224 | tf_op jit(solution)/shard_map/ppermute | solution.py:15
  20.8 3.4 %collective-permute-start.6 = (bf16[128,512]{1,0:T(8,128)(2,1)S(1)}, bf16[128,512]{1,0:T(8,128)(2,1)S(1)}, u32[]{:S(2)}, u32[]{:S(2)}) collective-permute-start(bf16[128,512]{1,0:T(8,128)(2,1)S(1)} %collective-permute-done.5.refs_6_), channel_id=1, source_target_pairs={{0,7},{1,0},{2,1},{3,2},{4,3},{5,4},{6,5},{7,6},{8,15},{9,8},{10,9... | collective-permute-start | bytes 393224 | tf_op jit(solution)/shard_map/ppermute | solution.py:15
  24.3 3.3 %collective-permute-start.15 = (bf16[128,512]{1,0:T(8,128)(2,1)S(1)}, bf16[128,512]{1,0:T(8,128)(2,1)S(1)}, u32[]{:S(2)}, u32[]{:S(2)}) collective-permute-start(bf16[128,512]{1,0:T(8,128)(2,1)S(1)} %collective-permute-done.14.refs_14_), channel_id=1, source_target_pairs={{0,7},{1,0},{2,1},{3,2},{4,3},{5,4},{6,5},{7,6},{8,15},{9,8},{10,9... | collective-permute-start | bytes 393224 | tf_op jit(solution)/shard_map/ppermute | solution.py:15
  27.6 3.4 %collective-permute-start.7 = (bf16[64,512]{1,0:T(8,128)(2,1)S(1)}, bf16[64,512]{1,0:T(8,128)(2,1)S(1)}, u32[]{:S(2)}, u32[]{:S(2)}) collective-permute-start(bf16[64,512]{1,0:T(8,128)(2,1)S(1)} %slice.61), channel_id=1, source_target_pairs={{0,7},{1,0},{2,1},{3,2},{4,3},{5,4},{6,5},{7,6},{8,15},{9,8},{10,9... | collective-permute-start | bytes 196616 | tf_op jit(solution)/shard_map/ppermute | solution.py:15
  31.7 3.3 %collective-permute-start.16 = (bf16[64,512]{1,0:T(8,128)(2,1)S(1)}, bf16[64,512]{1,0:T(8,128)(2,1)S(1)}, u32[]{:S(2)}, u32[]{:S(2)}) collective-permute-start(bf16[64,512]{1,0:T(8,128)(2,1)S(1)} %slice.63), channel_id=1, source_target_pairs={{0,7},{1,0},{2,1},{3,2},{4,3},{5,4},{6,5},{7,6},{8,15},{9,8},{10,9... | collective-permute-start | bytes 196616 | tf_op jit(solution)/shard_map/ppermute | solution.py:15
  35.3 1.3 collective-permute-done.3
  37.3 3.5 %collective-permute-done.12 = bf16[64,512]{1,0:T(8,128)(2,1)S(1)} collective-permute-done((bf16[64,512]{1,0:T(8,128)(2,1)S(1)}, bf16[64,512]{1,0:T(8,128)(2,1)S(1)}, u32[]{:S(2)}, u32[]{:S(2)}) %collective-permute-start.12) | collective-permute-done | bytes 65568 | tf_op jit(solution)/shard_map/ppermute | solution.py:15
  41.5 65.6 %place.1 = (bf16[1024,512]{1,0:T(8,128)(2,1)}, bf16[1024,512]{1,0:T(8,128)(2,1)}) custom-call(s32[16]{0:T(128)} %fusion.41.spot_ref, bf16[128,512]{1,0:T(8,128)(2,1)} %copy-done.10, bf16[128,512]{1,0:T(8,128)(2,1)} %copy-done.14, bf16[128,512]{1,0:T(8,128)(2,1)} %copy-done.18, bf16[128,512]{1,0:T(8,128)(2,1)} %copy-done.7, ...), custom_call_target="tpu_custom_call" | custom-call | tf_op jit(solution)/shard_map/place/pallas_call | solution.py:63
  107.2 2.1 fusion.21
  109.4 1.0 fusion.18
  110.9 0.9 fusion.24
  114.4 3.5 %collective-permute-done.17 = bf16[512,3072]{1,0:T(8,128)(2,1)S(1)} collective-permute-done((bf16[512,3072]{1,0:T(8,128)(2,1)S(1)}, bf16[512,3072]{1,0:T(8,128)(2,1)S(1)}, u32[]{:S(2)}, u32[]{:S(2)}) %collective-permute-start.17) | collective-permute-done | bytes 3145760 | tf_op jit(solution)/shard_map/ppermute | solution.py:15
  117.8 4.7 %fusion.9 = bf16[512,3072]{1,0:T(8,128)(2,1)S(1)} fusion(bf16[512,3072]{1,0:T(8,128)(2,1)S(1)} %collective-permute-done.17, f32[512,1024]{1,0:T(8,128)S(1)} %fusion.31, f32[512,1024]{1,0:T(8,128)S(1)} %fusion.35, f32[512,1024]{1,0:T(8,128)S(1)} %fusion.37), kind=kLoop, calls=%fused_computation.24 | loop fusion | flops 33030144 | bytes 12582912 | tf_op jit(solution)/shard_map/convert_element_type | solution.py:32
  122.5 45.4 %all_to_all.27 = bf16[8,64,3072]{2,1,0:T(8,128)(2,1)S(1)} all-to-all(bf16[8,64,3072]{2,1,0:T(8,128)(2,1)S(1)} %bitcast.16), channel_id=1, replica_groups=mesh['y'=4,'h'=2,'c'=2,'l'=2,'z'=8] {'y','h'}, dimensions={0} | all-to-all | bytes 6291456 | tf_op jit(solution)/shard_map/all_to_all | solution.py:102
  167.9 3.0 %fusion.15 = f32[64,3072]{1,0:T(8,128)S(1)} fusion(bf16[8,64,3072]{2,1,0:T(8,128)(2,1)S(1)} %all_to_all.27), kind=kLoop, calls=%fused_computation.30 | loop fusion | flops 17104896 | bytes 3932160 | tf_op jit(solution)/shard_map/reduce_sum | solution.py:103
  171.5 42.0 %all_to_all.28 = bf16[8,64,3072]{2,1,0:T(8,128)(2,1)} all-to-all(bf16[8,64,3072]{2,1,0:T(8,128)(2,1)S(1)} %broadcast_in_dim.5), channel_id=1, replica_groups=mesh['y'=4,'h'=2,'c'=2,'l'=2,'z'=8] {'y','h'}, dimensions={0} | all-to-all | bytes 6291456 | tf_op jit(solution)/shard_map/all_to_all | solution.py:111
  213.5 6.0 %collective-permute-done.18 = bf16[512,3072]{1,0:T(8,128)(2,1)} collective-permute-done((bf16[512,3072]{1,0:T(8,128)(2,1)}, bf16[512,3072]{1,0:T(8,128)(2,1)}, u32[]{:S(2)}, u32[]{:S(2)}) %collective-permute-start.18) | collective-permute-done | bytes 3145760 | tf_op jit(solution)/shard_map/ppermute | solution.py:15
  219.5 1.7 fusion.25
  221.3 1.3 fusion.52
  222.6 2.8 %add_convert_fusion = bf16[1024,512]{1,0:T(8,128)(2,1)S(1)} fusion(f32[1024,512]{1,0:T(8,128)S(1)} %fusion.52, bf16[512,1024]{1,0:T(8,128)(2,1)S(1)} %copy-done.2, bf16[512,3072]{1,0:T(8,128)(2,1)} %bitcast.1, bf16[512,3072]{1,0:T(8,128)(2,1)} %collective-permute-done.18), kind=kOutput, calls=%fused_computation.50 | convolution fusion | flops 1078984704 | bytes 10485760 | tf_op jit(solution)/shard_map/dot_general | solution.py:79
  225.5 2.4 fusion.29
  227.9 4.3 %all-to-all-start.2 = ((bf16[16,64,512]{2,1,0:T(8,128)(2,1)}), bf16[16,64,512]{2,1,0:T(8,128)(2,1)}, u32[]{:S(2)}, u32[]{:S(2)}) async-start(bf16[16,64,512]{2,1,0:T(8,128)(2,1)} %bitcast.17), calls=%async_computation.2 | async-start | bytes 2097152 | tf_op jit(solution)/shard_map/all_to_all | solution.py:119
  232.2 4.6 %fusion.27 = f32[1024,512]{1,0:T(8,128)} fusion(bf16[1024,512]{1,0:T(8,128)(2,1)} %get-tuple-element.7, bf16[512,3072]{1,0:T(8,128)(2,1)} %collective-permute-done.18, bf16[512,3072]{1,0:T(8,128)(2,1)} %bitcast.1), kind=kOutput, calls=%fused_computation.47 | convolution fusion | flops 1077936128 | bytes 9437184 | tf_op jit(solution)/shard_map/dot_general | solution.py:83
  236.8 2.6 fusion.53
  239.4 4.2 %fusion.49 = f32[512,1024]{1,0:T(8,128)} fusion(bf16[1024,512]{1,0:T(8,128)(2,1)S(1)} %copy-done.4, bf16[512,3072]{1,0:T(8,128)(2,1)} %bitcast.1, bf16[512,3072]{1,0:T(8,128)(2,1)} %collective-permute-done.18), kind=kOutput, calls=%fused_computation.96 | convolution fusion | flops 1077936128 | bytes 9437184 | tf_op jit(solution)/shard_map/dot_general | solution.py:83
  243.6 16.4 %all-to-all-done.2 = bf16[16,64,512]{2,1,0:T(8,128)(2,1)} async-done(((bf16[16,64,512]{2,1,0:T(8,128)(2,1)}), bf16[16,64,512]{2,1,0:T(8,128)(2,1)}, u32[]{:S(2)}, u32[]{:S(2)}) %all-to-all-start.2) | async-done | bytes 1048608 | tf_op jit(solution)/shard_map/all_to_all | solution.py:119
  260.0 2.0 convert_reduce_fusion
  (83 shorter events, 7.2 us)
Async XLA Ops:
  0.6 106.5 %copy-start = (bf16[512,1024]{1,0:T(8,128)(2,1)S(1)}, bf16[512,1024]{1,0:T(8,128)(2,1)}, u32[]{:S(2)}) copy-start(bf16[512,1024]{1,0:T(8,128)(2,1)} %param.8) | copy-start | bytes 3145732
  2.4 39.0 %copy-start.10 = (bf16[128,512]{1,0:T(8,128)(2,1)}, bf16[128,512]{1,0:T(8,128)(2,1)S(1)}, u32[]{:S(2)}) copy-start(bf16[128,512]{1,0:T(8,128)(2,1)S(1)} %constant_dynamic-update-slice_fusion.refs_0_) | copy-start | bytes 393220
  2.4 7.4 %collective-permute-start.8 = (bf16[128,512]{1,0:T(8,128)(2,1)S(1)}, bf16[128,512]{1,0:T(8,128)(2,1)S(1)}, u32[]{:S(2)}, u32[]{:S(2)}) collective-permute-start(bf16[128,512]{1,0:T(8,128)(2,1)S(1)} %constant_dynamic-update-slice_fusion.refs_0_), channel_id=1, source_target_pairs={{0,8},{8,0},{1,9},{9,1},{2,10},{10,2},{3,11},{11,3},{4,12},{12,4},... | collective-permute-start | bytes 393224 | tf_op jit(solution)/shard_map/ppermute | solution.py:15
  3.9 9.6 %collective-permute-start.4 = (bf16[128,512]{1,0:T(8,128)(2,1)S(1)}, bf16[128,512]{1,0:T(8,128)(2,1)S(1)}, u32[]{:S(2)}, u32[]{:S(2)}) collective-permute-start(bf16[128,512]{1,0:T(8,128)(2,1)S(1)} %constant_dynamic-update-slice_fusion.refs_0_), channel_id=1, source_target_pairs={{0,7},{1,0},{2,1},{3,2},{4,3},{5,4},{6,5},{7,6},{8,15},{9,8},{10,9... | collective-permute-start | bytes 393224 | tf_op jit(solution)/shard_map/ppermute | solution.py:15
  9.8 7.0 %collective-permute-start = (bf16[128,512]{1,0:T(8,128)(2,1)S(1)}, bf16[128,512]{1,0:T(8,128)(2,1)S(1)}, u32[]{:S(2)}, u32[]{:S(2)}) collective-permute-start(bf16[128,512]{1,0:T(8,128)(2,1)S(1)} %constant_dynamic-update-slice_fusion.refs_0_), channel_id=1, source_target_pairs={{0,1},{1,2},{2,3},{3,4},{4,5},{5,6},{6,7},{7,0},{8,9},{9,10},{10,1... | collective-permute-start | bytes 393224 | tf_op jit(solution)/shard_map/ppermute | solution.py:15
  9.8 31.7 %copy-start.12 = (bf16[128,512]{1,0:T(8,128)(2,1)}, bf16[128,512]{1,0:T(8,128)(2,1)S(1)}, u32[]{:S(2)}) copy-start(bf16[128,512]{1,0:T(8,128)(2,1)S(1)} %collective-permute-done.8.refs_8_) | copy-start | bytes 393220
  9.8 7.0 %collective-permute-start.13 = (bf16[128,512]{1,0:T(8,128)(2,1)S(1)}, bf16[128,512]{1,0:T(8,128)(2,1)S(1)}, u32[]{:S(2)}, u32[]{:S(2)}) collective-permute-start(bf16[128,512]{1,0:T(8,128)(2,1)S(1)} %collective-permute-done.8.refs_8_), channel_id=1, source_target_pairs={{0,7},{1,0},{2,1},{3,2},{4,3},{5,4},{6,5},{7,6},{8,15},{9,8},{10,9... | collective-permute-start | bytes 393224 | tf_op jit(solution)/shard_map/ppermute | solution.py:15
  13.5 7.3 %collective-permute-start.9 = (bf16[128,512]{1,0:T(8,128)(2,1)S(1)}, bf16[128,512]{1,0:T(8,128)(2,1)S(1)}, u32[]{:S(2)}, u32[]{:S(2)}) collective-permute-start(bf16[128,512]{1,0:T(8,128)(2,1)S(1)} %collective-permute-done.8.refs_8_), channel_id=1, source_target_pairs={{0,1},{1,2},{2,3},{3,4},{4,5},{5,6},{6,7},{7,0},{8,9},{9,10},{10,1... | collective-permute-start | bytes 393224 | tf_op jit(solution)/shard_map/ppermute | solution.py:15
  13.5 27.9 %copy-start.13 = (bf16[128,512]{1,0:T(8,128)(2,1)}, bf16[128,512]{1,0:T(8,128)(2,1)S(1)}, u32[]{:S(2)}) copy-start(bf16[128,512]{1,0:T(8,128)(2,1)S(1)} %collective-permute-done.4.refs_7_) | copy-start | bytes 393220
  13.5 7.3 %collective-permute-start.5 = (bf16[128,512]{1,0:T(8,128)(2,1)S(1)}, bf16[128,512]{1,0:T(8,128)(2,1)S(1)}, u32[]{:S(2)}, u32[]{:S(2)}) collective-permute-start(bf16[128,512]{1,0:T(8,128)(2,1)S(1)} %collective-permute-done.4.refs_7_), channel_id=1, source_target_pairs={{0,7},{1,0},{2,1},{3,2},{4,3},{5,4},{6,5},{7,6},{8,15},{9,8},{10,9... | collective-permute-start | bytes 393224 | tf_op jit(solution)/shard_map/ppermute | solution.py:15
  16.8 24.7 %copy-start.14 = (bf16[128,512]{1,0:T(8,128)(2,1)}, bf16[128,512]{1,0:T(8,128)(2,1)S(1)}, u32[]{:S(2)}) copy-start(bf16[128,512]{1,0:T(8,128)(2,1)S(1)} %collective-permute-done.refs_1_) | copy-start | bytes 393220
  16.8 7.5 %collective-permute-start.1 = (bf16[128,512]{1,0:T(8,128)(2,1)S(1)}, bf16[128,512]{1,0:T(8,128)(2,1)S(1)}, u32[]{:S(2)}, u32[]{:S(2)}) collective-permute-start(bf16[128,512]{1,0:T(8,128)(2,1)S(1)} %collective-permute-done.refs_1_), channel_id=1, source_target_pairs={{0,1},{1,2},{2,3},{3,4},{4,5},{5,6},{6,7},{7,0},{8,9},{9,10},{10,1... | collective-permute-start | bytes 393224 | tf_op jit(solution)/shard_map/ppermute | solution.py:15
  16.8 24.7 %copy-start.15 = (bf16[128,512]{1,0:T(8,128)(2,1)}, bf16[128,512]{1,0:T(8,128)(2,1)S(1)}, u32[]{:S(2)}) copy-start(bf16[128,512]{1,0:T(8,128)(2,1)S(1)} %collective-permute-done.13.refs_15_) | copy-start | bytes 393220
  16.8 7.4 %collective-permute-start.14 = (bf16[128,512]{1,0:T(8,128)(2,1)S(1)}, bf16[128,512]{1,0:T(8,128)(2,1)S(1)}, u32[]{:S(2)}, u32[]{:S(2)}) collective-permute-start(bf16[128,512]{1,0:T(8,128)(2,1)S(1)} %collective-permute-done.13.refs_15_), channel_id=1, source_target_pairs={{0,7},{1,0},{2,1},{3,2},{4,3},{5,4},{6,5},{7,6},{8,15},{9,8},{10,9... | collective-permute-start | bytes 393224 | tf_op jit(solution)/shard_map/ppermute | solution.py:15
  20.8 20.7 %copy-start.16 = (bf16[128,512]{1,0:T(8,128)(2,1)}, bf16[128,512]{1,0:T(8,128)(2,1)S(1)}, u32[]{:S(2)}) copy-start(bf16[128,512]{1,0:T(8,128)(2,1)S(1)} %collective-permute-done.9.refs_9_) | copy-start | bytes 393220
  20.8 6.8 %collective-permute-start.10 = (bf16[128,512]{1,0:T(8,128)(2,1)S(1)}, bf16[128,512]{1,0:T(8,128)(2,1)S(1)}, u32[]{:S(2)}, u32[]{:S(2)}) collective-permute-start(bf16[128,512]{1,0:T(8,128)(2,1)S(1)} %collective-permute-done.9.refs_9_), channel_id=1, source_target_pairs={{0,1},{1,2},{2,3},{3,4},{4,5},{5,6},{6,7},{7,0},{8,9},{9,10},{10,1... | collective-permute-start | bytes 393224 | tf_op jit(solution)/shard_map/ppermute | solution.py:15
  20.8 20.7 %copy-start.17 = (bf16[128,512]{1,0:T(8,128)(2,1)}, bf16[128,512]{1,0:T(8,128)(2,1)S(1)}, u32[]{:S(2)}) copy-start(bf16[128,512]{1,0:T(8,128)(2,1)S(1)} %collective-permute-done.5.refs_6_) | copy-start | bytes 393220
  20.8 6.8 %collective-permute-start.6 = (bf16[128,512]{1,0:T(8,128)(2,1)S(1)}, bf16[128,512]{1,0:T(8,128)(2,1)S(1)}, u32[]{:S(2)}, u32[]{:S(2)}) collective-permute-start(bf16[128,512]{1,0:T(8,128)(2,1)S(1)} %collective-permute-done.5.refs_6_), channel_id=1, source_target_pairs={{0,7},{1,0},{2,1},{3,2},{4,3},{5,4},{6,5},{7,6},{8,15},{9,8},{10,9... | collective-permute-start | bytes 393224 | tf_op jit(solution)/shard_map/ppermute | solution.py:15
  24.2 17.2 %copy-start.18 = (bf16[128,512]{1,0:T(8,128)(2,1)}, bf16[128,512]{1,0:T(8,128)(2,1)S(1)}, u32[]{:S(2)}) copy-start(bf16[128,512]{1,0:T(8,128)(2,1)S(1)} %collective-permute-done.1.refs_2_) | copy-start | bytes 393220
  24.2 6.8 %collective-permute-start.2 = (bf16[128,512]{1,0:T(8,128)(2,1)S(1)}, bf16[128,512]{1,0:T(8,128)(2,1)S(1)}, u32[]{:S(2)}, u32[]{:S(2)}) collective-permute-start(bf16[128,512]{1,0:T(8,128)(2,1)S(1)} %collective-permute-done.1.refs_2_), channel_id=1, source_target_pairs={{0,1},{1,2},{2,3},{3,4},{4,5},{5,6},{6,7},{7,0},{8,9},{9,10},{10,1... | collective-permute-start | bytes 393224 | tf_op jit(solution)/shard_map/ppermute | solution.py:15
  24.2 17.2 %copy-start.19 = (bf16[128,512]{1,0:T(8,128)(2,1)}, bf16[128,512]{1,0:T(8,128)(2,1)S(1)}, u32[]{:S(2)}) copy-start(bf16[128,512]{1,0:T(8,128)(2,1)S(1)} %collective-permute-done.14.refs_14_) | copy-start | bytes 393220
  24.3 7.4 %collective-permute-start.15 = (bf16[128,512]{1,0:T(8,128)(2,1)S(1)}, bf16[128,512]{1,0:T(8,128)(2,1)S(1)}, u32[]{:S(2)}, u32[]{:S(2)}) collective-permute-start(bf16[128,512]{1,0:T(8,128)(2,1)S(1)} %collective-permute-done.14.refs_14_), channel_id=1, source_target_pairs={{0,7},{1,0},{2,1},{3,2},{4,3},{5,4},{6,5},{7,6},{8,15},{9,8},{10,9... | collective-permute-start | bytes 393224 | tf_op jit(solution)/shard_map/ppermute | solution.py:15
  27.5 13.9 %copy-start.20 = (bf16[128,512]{1,0:T(8,128)(2,1)}, bf16[128,512]{1,0:T(8,128)(2,1)S(1)}, u32[]{:S(2)}) copy-start(bf16[128,512]{1,0:T(8,128)(2,1)S(1)} %collective-permute-done.10.refs_10_) | copy-start | bytes 393220
  27.5 7.5 %collective-permute-start.11 = (bf16[128,512]{1,0:T(8,128)(2,1)S(1)}, bf16[128,512]{1,0:T(8,128)(2,1)S(1)}, u32[]{:S(2)}, u32[]{:S(2)}) collective-permute-start(bf16[128,512]{1,0:T(8,128)(2,1)S(1)} %collective-permute-done.10.refs_10_), channel_id=1, source_target_pairs={{0,1},{1,2},{2,3},{3,4},{4,5},{5,6},{6,7},{7,0},{8,9},{9,10},{10,1... | collective-permute-start | bytes 393224 | tf_op jit(solution)/shard_map/ppermute | solution.py:15
  27.6 13.9 %copy-start.6 = (bf16[128,512]{1,0:T(8,128)(2,1)}, bf16[128,512]{1,0:T(8,128)(2,1)S(1)}, u32[]{:S(2)}) copy-start(bf16[128,512]{1,0:T(8,128)(2,1)S(1)} %collective-permute-done.6.refs_5_) | copy-start | bytes 393220
  27.6 7.7 %collective-permute-start.7 = (bf16[64,512]{1,0:T(8,128)(2,1)S(1)}, bf16[64,512]{1,0:T(8,128)(2,1)S(1)}, u32[]{:S(2)}, u32[]{:S(2)}) collective-permute-start(bf16[64,512]{1,0:T(8,128)(2,1)S(1)} %slice.61), channel_id=1, source_target_pairs={{0,7},{1,0},{2,1},{3,2},{4,3},{5,4},{6,5},{7,6},{8,15},{9,8},{10,9... | collective-permute-start | bytes 196616 | tf_op jit(solution)/shard_map/ppermute | solution.py:15
  31.1 5.6 %collective-permute-start.3 = (bf16[64,512]{1,0:T(8,128)(2,1)S(1)}, bf16[64,512]{1,0:T(8,128)(2,1)S(1)}, u32[]{:S(2)}, u32[]{:S(2)}) collective-permute-start(bf16[64,512]{1,0:T(8,128)(2,1)S(1)} %slice.60), channel_id=1, source_target_pairs={{0,1},{1,2},{2,3},{3,4},{4,5},{5,6},{6,7},{7,0},{8,9},{9,10},{10,1... | collective-permute-start | bytes 196616 | tf_op jit(solution)/shard_map/ppermute | solution.py:15
  31.7 5.6 %collective-permute-start.16 = (bf16[64,512]{1,0:T(8,128)(2,1)S(1)}, bf16[64,512]{1,0:T(8,128)(2,1)S(1)}, u32[]{:S(2)}, u32[]{:S(2)}) collective-permute-start(bf16[64,512]{1,0:T(8,128)(2,1)S(1)} %slice.63), channel_id=1, source_target_pairs={{0,7},{1,0},{2,1},{3,2},{4,3},{5,4},{6,5},{7,6},{8,15},{9,8},{10,9... | collective-permute-start | bytes 196616 | tf_op jit(solution)/shard_map/ppermute | solution.py:15
  35.0 5.7 %collective-permute-start.12 = (bf16[64,512]{1,0:T(8,128)(2,1)S(1)}, bf16[64,512]{1,0:T(8,128)(2,1)S(1)}, u32[]{:S(2)}, u32[]{:S(2)}) collective-permute-start(bf16[64,512]{1,0:T(8,128)(2,1)S(1)} %slice.62), channel_id=1, source_target_pairs={{0,1},{1,2},{2,3},{3,4},{4,5},{5,6},{6,7},{7,0},{8,9},{9,10},{10,1... | collective-permute-start | bytes 196616 | tf_op jit(solution)/shard_map/ppermute | solution.py:15
  112.1 5.7 %collective-permute-start.17 = (bf16[512,3072]{1,0:T(8,128)(2,1)S(1)}, bf16[512,3072]{1,0:T(8,128)(2,1)S(1)}, u32[]{:S(2)}, u32[]{:S(2)}) collective-permute-start(bf16[512,3072]{1,0:T(8,128)(2,1)S(1)} %pad_maximum_fusion), channel_id=1, source_target_pairs={{0,16},{16,0},{1,17},{17,1},{2,18},{18,2},{3,19},{19,3},{4,20},{20... | collective-permute-start | bytes 9437192 | tf_op jit(solution)/shard_map/ppermute | solution.py:15
  213.5 6.0 %collective-permute-start.18 = (bf16[512,3072]{1,0:T(8,128)(2,1)}, bf16[512,3072]{1,0:T(8,128)(2,1)}, u32[]{:S(2)}, u32[]{:S(2)}) collective-permute-start(bf16[512,3072]{1,0:T(8,128)(2,1)} %bitcast.1), channel_id=1, source_target_pairs={{0,16},{16,0},{1,17},{17,1},{2,18},{18,2},{3,19},{19,3},{4,20},{20... | collective-permute-start | bytes 9437192 | tf_op jit(solution)/shard_map/ppermute | solution.py:15
  227.9 32.1 %all-to-all-start.2 = ((bf16[16,64,512]{2,1,0:T(8,128)(2,1)}), bf16[16,64,512]{2,1,0:T(8,128)(2,1)}, u32[]{:S(2)}, u32[]{:S(2)}) async-start(bf16[16,64,512]{2,1,0:T(8,128)(2,1)} %bitcast.17), calls=%async_computation.2 | async-start | bytes 2097152 | tf_op jit(solution)/shard_map/all_to_all | solution.py:119
  (9 other events, 39.8 us)
